TPU v7x, 32 devices: a whole 2x2x4 slice. The times are simulated.
32 devices in a mesh: dp: 4 (over y, core), fsdp: 8 (over z, x).
Axes of the slice: x: 2, y: 2, z: 4, core: 2. Of those that a mesh axis runs over, the one named last changes fastest.
Arguments:
- inputs: bfloat16 [128, 392, 512], P(('dp', 'fsdp')), may hold values from -6 to 6
- extents: int32 [128, 3], P(('dp', 'fsdp')), may hold values from 1 to 8, as said below
- cotangent: bfloat16 [128, 392, 512], P(('dp', 'fsdp')), may hold values from -6 to 6
- ln1_gain: bfloat16 [512], P(('dp', 'fsdp')), may hold values from 0.25 to 1.75
- ln1_shift: bfloat16 [512], P(('dp', 'fsdp')), may hold values from -3 to 3
- qkv_weight: bfloat16 [512, 1536], P(('dp', 'fsdp')), may hold values from -0.25 to 0.25
- query_bias: bfloat16 [512], P(('dp', 'fsdp')), may hold values from -3 to 3
- value_bias: bfloat16 [512], P(('dp', 'fsdp')), may hold values from -3 to 3
- bias_table: bfloat16 [2535, 16], replicated, may hold values from -4 to 4
- proj_weight: bfloat16 [512, 512], P(('dp', 'fsdp')), may hold values from -2 to 2
- proj_shift: bfloat16 [512], P(('dp', 'fsdp')), may hold values from -3 to 3
- ln2_gain: bfloat16 [512], P(('dp', 'fsdp')), may hold values from 0.25 to 1.75
- ln2_shift: bfloat16 [512], P(('dp', 'fsdp')), may hold values from -3 to 3
- fc1_weight: bfloat16 [512, 2048], P(('dp', 'fsdp')), may hold values from -0.25 to 0.25
- fc1_shift: bfloat16 [2048], P(('dp', 'fsdp')), may hold values from -3 to 3
- fc2_weight: bfloat16 [2048, 512], P(('dp', 'fsdp')), may hold values from -0.125 to 0.125
- fc2_shift: bfloat16 [512], P(('dp', 'fsdp')), may hold values from -3 to 3
Outputs:
- output: bfloat16 [128, 392, 512], P(('dp', 'fsdp'))
- input_grad: bfloat16 [128, 392, 512], P(('dp', 'fsdp'))
- ln1_gain_grad: float32 [512], P(('dp', 'fsdp'))
- ln1_shift_grad: float32 [512], P(('dp', 'fsdp'))
- qkv_weight_grad: float32 [512, 1536], P(('dp', 'fsdp'))
- query_bias_grad: float32 [512], P(('dp', 'fsdp'))
- value_bias_grad: float32 [512], P(('dp', 'fsdp'))
- bias_table_grad: float32 [2535, 16], replicated
- proj_weight_grad: float32 [512, 512], P(('dp', 'fsdp'))
- proj_shift_grad: float32 [512], P(('dp', 'fsdp'))
- ln2_gain_grad: float32 [512], P(('dp', 'fsdp'))
- ln2_shift_grad: float32 [512], P(('dp', 'fsdp'))
- fc1_weight_grad: float32 [512, 2048], P(('dp', 'fsdp'))
- fc1_shift_grad: float32 [2048], P(('dp', 'fsdp'))
- fc2_weight_grad: float32 [2048, 512], P(('dp', 'fsdp'))
- fc2_shift_grad: float32 [512], P(('dp', 'fsdp'))
Inputs may be any that keep to these rules, and one draw needn't show every extreme that they name: `extents`: each row gives a window's valid frames, patch rows and patch columns, each at least 1 and at most the window's extent along it; the first window of the whole array is complete.
All inputs are finite; a program needn't handle non-finite values.
Results may differ from a plain program's by a relative error of at most 0.012.
Values may be sent and summed in bfloat16 or wider, within the bound.
A program may use at most 448 MiB of HBM per device.

v0:
```python
import jax
import jax.numpy as jnp
from jax import lax
from jax.sharding import PartitionSpec as P

D = 512
HEADS = 16
HDIM = 32
WIN_T = 8
WIN_H = 7
WIN_W = 7


EPS = 1e-05
HIGHEST = lax.Precision.HIGHEST


def positions():
    spots = jnp.arange(WIN_T * WIN_H * WIN_W, dtype=jnp.int32)
    return (spots // (WIN_H * WIN_W), spots // WIN_W % WIN_H, spots % WIN_W)


def offset_onehot(extent):
    spots = jnp.arange(extent, dtype=jnp.int32)
    offset = spots[:, None] - spots[None, :] + extent - 1
    slots = jnp.arange(2 * extent - 1, dtype=jnp.int32)
    return (offset[:, :, None] == slots[None, None, :]).astype(jnp.float32)


def expand_bias(bias_table):
    table = bias_table.astype(jnp.float32).reshape(
        2 * WIN_T - 1, 2 * WIN_H - 1, 2 * WIN_W - 1, HEADS
    )
    first = jnp.einsum("tua,abeh->tubeh", offset_onehot(WIN_T), table, precision=HIGHEST)
    second = jnp.einsum("rvb,tubeh->turveh", offset_onehot(WIN_H), first, precision=HIGHEST)
    third = jnp.einsum("cwe,turveh->htrcuvw", offset_onehot(WIN_W), second, precision=HIGHEST)
    tokens = WIN_T * WIN_H * WIN_W
    return third.reshape(HEADS, tokens, tokens)


def fold_bias(bias_grad):
    spread = bias_grad.reshape(HEADS, WIN_T, WIN_H, WIN_W, WIN_T, WIN_H, WIN_W)
    first = jnp.einsum("cwe,htrcuvw->htruve", offset_onehot(WIN_W), spread, precision=HIGHEST)
    second = jnp.einsum("rvb,htruve->htube", offset_onehot(WIN_H), first, precision=HIGHEST)
    third = jnp.einsum("tua,htube->abeh", offset_onehot(WIN_T), second, precision=HIGHEST)
    return third.reshape(-1, HEADS)


def valid_mask(extents):
    depth, height, across = positions()
    return (
        (depth[None, :] < extents[:, 0:1])
        & (height[None, :] < extents[:, 1:2])
        & (across[None, :] < extents[:, 2:3])
    ).astype(jnp.float32)


def layer_norm(values, gain_vec, shift_vec):
    average = jnp.mean(values, axis=-1, keepdims=True)
    centered = values - average
    variance = jnp.mean(centered * centered, axis=-1, keepdims=True)
    return centered * lax.rsqrt(variance + EPS) * gain_vec + shift_vec


def exact_gelu(values):
    return jax.nn.gelu(values, approximate=False)


def matmul(left, right):
    return jnp.dot(left, right, preferred_element_type=jnp.float32)


def outer_sum(left, right):
    return lax.dot_general(
        left, right, (((0,), (0,)), ((), ())), preferred_element_type=jnp.float32
    )


def times_trans(left, right):
    return lax.dot_general(
        left, right, (((1,), (1,)), ((), ())), preferred_element_type=jnp.float32
    )


def attention_scores(qkv_block, keep, bias):
    count = qkv_block.shape[0]
    split = qkv_block.reshape(count, WIN_T * WIN_H * WIN_W, 3, HEADS, HDIM)
    queries = split[:, :, 0]
    key_part = split[:, :, 1]
    values = split[:, :, 2]
    scores = jnp.einsum(
        "gqhd,gkhd->ghqk", queries, key_part, preferred_element_type=jnp.float32
    ) * HDIM ** (-0.5)
    scores = scores + bias[None]
    scores = jnp.where(keep[:, None, None, :] > 0, scores, -jnp.inf)
    return (scores, queries, key_part, values)


def per_device(
    inputs,
    extents,
    cotangent,
    ln1_gain,
    ln1_shift,
    qkv_weight,
    query_bias,
    value_bias,
    bias_table,
    proj_weight,
    proj_shift,
    ln2_gain,
    ln2_shift,
    fc1_weight,
    fc1_shift,
    fc2_weight,
    fc2_shift,
):
    first_set = (
        lax.all_gather(ln1_gain, ("dp", "fsdp"), axis=0, tiled=True),
        lax.all_gather(ln1_shift, ("dp", "fsdp"), axis=0, tiled=True),
        lax.all_gather(qkv_weight, ("dp", "fsdp"), axis=0, tiled=True),
        lax.all_gather(query_bias, ("dp", "fsdp"), axis=0, tiled=True),
        lax.all_gather(value_bias, ("dp", "fsdp"), axis=0, tiled=True),
        lax.all_gather(proj_weight, ("dp", "fsdp"), axis=0, tiled=True),
        lax.all_gather(proj_shift, ("dp", "fsdp"), axis=0, tiled=True),
    )
    second_set = (
        lax.all_gather(ln2_gain, ("dp", "fsdp"), axis=0, tiled=True),
        lax.all_gather(ln2_shift, ("dp", "fsdp"), axis=0, tiled=True),
        lax.all_gather(fc1_weight, ("dp", "fsdp"), axis=0, tiled=True),
        lax.all_gather(fc1_shift, ("dp", "fsdp"), axis=0, tiled=True),
        lax.all_gather(fc2_weight, ("dp", "fsdp"), axis=0, tiled=True),
        lax.all_gather(fc2_shift, ("dp", "fsdp"), axis=0, tiled=True),
    )
    gain_one, shift_one, qkv_full, qbias_full, vbias_full, proj_full, pshift_full = first_set
    gain_two, shift_two, fc1_full, fshift_one, fc2_full, fshift_two = second_set
    windows = inputs.shape[0]
    tokens = WIN_T * WIN_H * WIN_W
    rows = inputs.reshape(windows * tokens, D).astype(jnp.float32)
    keep = valid_mask(extents)
    keep_rows = keep.reshape(-1, 1)
    bias = expand_bias(bias_table)
    normed_one, back_one = jax.vjp(
        layer_norm, rows, gain_one.astype(jnp.float32), shift_one.astype(jnp.float32)
    )
    normed_one = normed_one.astype(jnp.bfloat16)
    qkv_shift = jnp.concatenate([qbias_full, jnp.zeros_like(qbias_full), vbias_full]).astype(
        jnp.float32
    )
    qkv_rows = (
        (matmul(normed_one, qkv_full) + qkv_shift)
        .astype(jnp.bfloat16)
        .reshape(windows, tokens, 3 * D)
    )
    scores, queries, key_part, values = attention_scores(qkv_rows, keep, bias)
    top = jnp.max(scores, axis=-1, keepdims=True)
    expo = jnp.exp(scores - top)
    total = jnp.sum(expo, axis=-1, keepdims=True)
    log_total = top + jnp.log(total)
    probs = (expo / total).astype(jnp.bfloat16)
    mixed = jnp.einsum("ghqk,gkhd->gqhd", probs, values, preferred_element_type=jnp.float32)
    attended = mixed.reshape(windows * tokens, D).astype(jnp.bfloat16)
    resid = rows + (matmul(attended, proj_full) + pshift_full.astype(jnp.float32))
    normed_two, back_two = jax.vjp(
        layer_norm, resid, gain_two.astype(jnp.float32), shift_two.astype(jnp.float32)
    )
    normed_two = normed_two.astype(jnp.bfloat16)
    hidden = matmul(normed_two, fc1_full) + fshift_one.astype(jnp.float32)
    active, gelu_back = jax.vjp(exact_gelu, hidden)
    active = active.astype(jnp.bfloat16)
    out_rows = (resid + (matmul(active, fc2_full) + fshift_two.astype(jnp.float32))) * keep_rows
    output = out_rows.astype(jnp.bfloat16).reshape(inputs.shape)
    second_back = (
        lax.all_gather(ln2_gain, ("dp", "fsdp"), axis=0, tiled=True),
        lax.all_gather(ln2_shift, ("dp", "fsdp"), axis=0, tiled=True),
        lax.all_gather(fc1_weight, ("dp", "fsdp"), axis=0, tiled=True),
        lax.all_gather(fc1_shift, ("dp", "fsdp"), axis=0, tiled=True),
        lax.all_gather(fc2_weight, ("dp", "fsdp"), axis=0, tiled=True),
        lax.all_gather(fc2_shift, ("dp", "fsdp"), axis=0, tiled=True),
    )
    fc1_back = second_back[2]
    fc2_back = second_back[4]
    grad_out = cotangent.reshape(windows * tokens, D).astype(jnp.float32) * keep_rows
    grad_low = grad_out.astype(jnp.bfloat16)
    fc2_grad = outer_sum(active, grad_low)
    fshift_two_grad = jnp.sum(grad_out, axis=0)
    (hidden_grad,) = gelu_back(times_trans(grad_low, fc2_back))
    hidden_low = hidden_grad.astype(jnp.bfloat16)
    fc1_grad = outer_sum(normed_two, hidden_low)
    fshift_one_grad = jnp.sum(hidden_low.astype(jnp.float32), axis=0)
    resid_ln, gain_two_grad, shift_two_grad = back_two(times_trans(hidden_low, fc1_back))
    resid_grad = grad_out + resid_ln
    first_back = (
        lax.all_gather(ln1_gain, ("dp", "fsdp"), axis=0, tiled=True),
        lax.all_gather(ln1_shift, ("dp", "fsdp"), axis=0, tiled=True),
        lax.all_gather(qkv_weight, ("dp", "fsdp"), axis=0, tiled=True),
        lax.all_gather(query_bias, ("dp", "fsdp"), axis=0, tiled=True),
        lax.all_gather(value_bias, ("dp", "fsdp"), axis=0, tiled=True),
        lax.all_gather(proj_weight, ("dp", "fsdp"), axis=0, tiled=True),
        lax.all_gather(proj_shift, ("dp", "fsdp"), axis=0, tiled=True),
    )
    qkv_back = first_back[2]
    proj_back = first_back[5]
    branch_low = resid_grad.astype(jnp.bfloat16)
    proj_grad = outer_sum(attended, branch_low)
    pshift_grad = jnp.sum(branch_low.astype(jnp.float32), axis=0)
    attended_grad = (
        times_trans(branch_low, proj_back)
        .astype(jnp.bfloat16)
        .reshape(windows, tokens, HEADS, HDIM)
    )
    scores, queries, key_part, values = attention_scores(qkv_rows, keep, bias)
    probs_full = jnp.exp(scores - log_total)
    probs_low = probs_full.astype(jnp.bfloat16)
    value_grad = jnp.einsum(
        "ghqk,gqhd->gkhd", probs_low, attended_grad, preferred_element_type=jnp.float32
    )
    probs_grad = jnp.einsum(
        "gqhd,gkhd->ghqk", attended_grad, values, preferred_element_type=jnp.float32
    )
    inner = jnp.sum(probs_grad * probs_full, axis=-1, keepdims=True)
    scores_grad = (probs_full * (probs_grad - inner)).astype(jnp.bfloat16)
    scale = HDIM ** (-0.5)
    query_grad = (
        jnp.einsum("ghqk,gkhd->gqhd", scores_grad, key_part, preferred_element_type=jnp.float32)
        * scale
    )
    key_grad = (
        jnp.einsum("ghqk,gqhd->gkhd", scores_grad, queries, preferred_element_type=jnp.float32)
        * scale
    )
    qkv_grad = jnp.stack([query_grad, key_grad, value_grad], axis=2).astype(jnp.bfloat16)
    qkv_grad = qkv_grad.reshape(windows * tokens, 3 * D)
    qkv_weight_grad = outer_sum(normed_one, qkv_grad)
    column_sums = jnp.sum(qkv_grad.astype(jnp.float32), axis=0)
    qbias_grad = column_sums[:D]
    vbias_grad = column_sums[2 * D :]
    rows_ln, gain_one_grad, shift_one_grad = back_one(times_trans(qkv_grad, qkv_back))
    input_grad = (resid_grad + rows_ln).astype(jnp.bfloat16).reshape(inputs.shape)
    bias_grad = jnp.sum(scores_grad.astype(jnp.float32), axis=0)
    table_local = fold_bias(bias_grad)
    table_grad = lax.psum(table_local, ("dp", "fsdp"))
    every_owned = (
        lax.psum_scatter(gain_one_grad, ("dp", "fsdp"), scatter_dimension=0, tiled=True),
        lax.psum_scatter(shift_one_grad, ("dp", "fsdp"), scatter_dimension=0, tiled=True),
        lax.psum_scatter(qkv_weight_grad, ("dp", "fsdp"), scatter_dimension=0, tiled=True),
        lax.psum_scatter(qbias_grad, ("dp", "fsdp"), scatter_dimension=0, tiled=True),
        lax.psum_scatter(vbias_grad, ("dp", "fsdp"), scatter_dimension=0, tiled=True),
        lax.psum_scatter(proj_grad, ("dp", "fsdp"), scatter_dimension=0, tiled=True),
        lax.psum_scatter(pshift_grad, ("dp", "fsdp"), scatter_dimension=0, tiled=True),
        lax.psum_scatter(gain_two_grad, ("dp", "fsdp"), scatter_dimension=0, tiled=True),
        lax.psum_scatter(shift_two_grad, ("dp", "fsdp"), scatter_dimension=0, tiled=True),
        lax.psum_scatter(fc1_grad, ("dp", "fsdp"), scatter_dimension=0, tiled=True),
        lax.psum_scatter(fshift_one_grad, ("dp", "fsdp"), scatter_dimension=0, tiled=True),
        lax.psum_scatter(fc2_grad, ("dp", "fsdp"), scatter_dimension=0, tiled=True),
        lax.psum_scatter(fshift_two_grad, ("dp", "fsdp"), scatter_dimension=0, tiled=True),
    )
    attn_owned = every_owned[:7]
    mlp_owned = every_owned[7:]
    return (
        output,
        input_grad,
        attn_owned[0],
        attn_owned[1],
        attn_owned[2],
        attn_owned[3],
        attn_owned[4],
        table_grad,
        attn_owned[5],
        attn_owned[6],
        mlp_owned[0],
        mlp_owned[1],
        mlp_owned[2],
        mlp_owned[3],
        mlp_owned[4],
        mlp_owned[5],
    )


def solution(mesh):
    in_specs = (
        P(("dp", "fsdp"), None, None),
        P(("dp", "fsdp"), None),
        P(("dp", "fsdp"), None, None),
        P(("dp", "fsdp")),
        P(("dp", "fsdp")),
        P(("dp", "fsdp"), None),
        P(("dp", "fsdp")),
        P(("dp", "fsdp")),
        P(),
        P(("dp", "fsdp"), None),
        P(("dp", "fsdp")),
        P(("dp", "fsdp")),
        P(("dp", "fsdp")),
        P(("dp", "fsdp"), None),
        P(("dp", "fsdp")),
        P(("dp", "fsdp"), None),
        P(("dp", "fsdp")),
    )
    out_specs = (
        P(("dp", "fsdp"), None, None),
        P(("dp", "fsdp"), None, None),
        P(("dp", "fsdp")),
        P(("dp", "fsdp")),
        P(("dp", "fsdp"), None),
        P(("dp", "fsdp")),
        P(("dp", "fsdp")),
        P(),
        P(("dp", "fsdp"), None),
        P(("dp", "fsdp")),
        P(("dp", "fsdp")),
        P(("dp", "fsdp")),
        P(("dp", "fsdp"), None),
        P(("dp", "fsdp")),
        P(("dp", "fsdp"), None),
        P(("dp", "fsdp")),
    )
    return jax.shard_map(
        per_device, mesh=mesh, in_specs=in_specs, out_specs=out_specs, check_vma=False
    )
```

profile of v0, /device:TPU:0, one launch (start us, length us, event | category | flops | bytes accessed | tf_op | source)
XLA Modules:
  0.0 1643.2 jit_solution(6884974490725847605)
XLA Ops:
  9.6 1.8 convert_reduce_fusion.4
  11.4 2.7 multiply_reduce_fusion.7
  18.1 42.5 %all-reduce.19 = (bf16[512]{0:T(512)(128)(2,1)}, bf16[512]{0:T(512)(128)(2,1)}, bf16[512]{0:T(512)(128)(2,1)}, bf16[512]{0:T(512)(128)(2,1)}, bf16[512]{0:T(512)...) all-reduce(bf16[512]{0:T(512)(128)(2,1)S(1)} %dynamic-update-slice., ...), channel_id=1, replica_groups=mesh['dp'=4,'fsdp'=8] {'dp','fsdp'}, use_global_device_ids=true, to_apply=%add.3 | all-reduce | flops 6144 | bytes 24576
  62.2 2.1 copy.62
  65.9 12.6 convolution_bitcast_fusion.2
  78.5 44.9 %convolution_bitcast_fusion = f32[16,8,7,7,8,7,7]{0,6,3,5,2,4,1:T(8,128)} fusion(f32[8,8,7,7,13,16,1]{5,3,2,4,1,0,6:T(8,128)} %convolution_bitcast_fusion.2, s32[7,7]{1,0:T(8,128)S(1)} %subtract_add_fusion), kind=kOutput, calls=%fused_computation.9 | convolution fusion | flops 383545984 | bytes 12443844 | tf_op jit(solution)/shard_map/cwe,turveh->htrcuvw/dot_general | solution.py:36
  123.4 59.4 %copy.65 = f32[16,8,7,7,8,7,7]{0,6,5,4,3,2,1:T(8,128)} copy(f32[16,8,7,7,8,7,7]{0,6,3,5,2,4,1:T(8,128)} %convolution_bitcast_fusion) | data formatting | bytes 19668992 | tf_op jit(solution)/shard_map/cwe,turveh->htrcuvw/transpose | solution.py:36
  182.8 85.6 %add.197 = f32[16,392,392]{0,2,1:T(8,128)} reshape(f32[16,8,7,7,8,7,7]{0,6,5,4,3,2,1:T(8,128)} %copy.65) | data formatting | bytes 19668992 | tf_op jit(solution)/shard_map/add | solution.py:94
  268.4 54.5 %copy.66 = f32[16,392,392]{1,2,0:T(8,128)} copy(f32[16,392,392]{0,2,1:T(8,128)} %add.197) | data formatting | bytes 19668992 | tf_op jit(solution)/shard_map/add | solution.py:94
  323.3 73.8 %all_gather.48 = bf16[512,512]{1,0:T(8,128)(2,1)} all-gather(bf16[16,512]{1,0:T(8,128)(2,1)S(1)} %copy-done.51), channel_id=1, replica_groups=mesh['dp'=4,'fsdp'=8] {'dp','fsdp'}, dimensions={0}, use_global_device_ids=true | all-gather | bytes 540672 | tf_op jit(solution)/shard_map/all_gather | solution.py:124
  397.4 1.5 fusion.15
  398.9 1.8 add_convert_fusion.2
  400.8 6.6 add_convert_fusion.1
  407.3 7.4 copy.58
  414.8 18.3 %reshape_reshape.4 = bf16[4,392,3,16,32]{1,0,4,3,2:T(4,128)(2,1)} reshape(bf16[1568,1536]{0,1:T(8,128)(2,1)} %copy.58) | data formatting | bytes 9633792 | tf_op jit(solution)/shard_map/reshape;reshape | solution.py:87
  433.1 5.3 fusion.59
  438.4 29.8 %fusion.61 = (f32[4,16,392]{2,1,0:T(8,128)S(1)}, f32[4,16,392,392]{2,3,1,0:T(8,128)}) fusion(f32[16,392,392]{1,2,0:T(8,128)} %copy.66, bf16[4,392,1,16,32]{1,0,4,3,2:T(4,128)(2,1)S(1)} %get-tuple-element.57, bf16[4,392,1,16,32]{1,0,4,3,2:T(4,128)(2,1)S(1)} %get-tuple-element.56, pred[4,392]{1,0:T(4,128)(4,1)S(1)} %get-tuple-element.53), kind=kOutput, calls=%fused_computation.132 | convolution fusion | flops 668720640 | bytes 52485664 | tf_op jit(solution)/shard_map/gqhd,gkhd->ghqk/dot_general | solution.py:91
  468.2 16.8 %fusion = f32[4,16,392]{2,1,0:T(8,128)S(1)} fusion(f32[4,16,392,392]{2,3,1,0:T(8,128)} %get-tuple-element.63, f32[4,16,392]{2,1,0:T(8,128)S(1)} %get-tuple-element.62), kind=kLoop, calls=%fused_computation.7 | loop fusion | flops 19643904 | bytes 39538688 | tf_op jit(solution)/shard_map/reduce_sum | solution.py:158
  485.7 19.4 %convert_bitcast_fusion = bf16[4,392,16,32]{1,3,2,0:T(8,128)(2,1)S(1)} fusion(f32[4,16,392,392]{2,3,1,0:T(8,128)} %get-tuple-element.63, f32[4,16,392]{2,1,0:T(8,128)S(1)} %fusion, f32[4,16,392]{2,1,0:T(8,128)S(1)} %get-tuple-element.62, bf16[4,392,1,16,32]{1,0,4,3,2:T(4,128)(2,1)} %get-tuple-element.55), kind=kOutput, calls=%fused_computation.68 | convolution fusion | flops 659714048 | bytes 42749952 | tf_op jit(solution)/shard_map/ghqk,gkhd->gqhd/dot_general | solution.py:161
  505.1 3.0 copy.68
  508.1 4.0 convert_element_type.165
  512.2 2.6 fusion.62
  514.9 1.7 copy-done.11
  517.3 35.1 %multiply_convert_fusion.1 = (bf16[1568,2048]{1,0:T(8,128)(2,1)}, f32[1568,2048]{1,0:T(8,128)}, f32[1568,2048]{1,0:T(8,128)}) fusion(f32[2048]{0:T(1024)S(1)} %convert_element_type.170, bf16[512,2048]{1,0:T(8,128)(2,1)} %all-gather.6.cloned.1.call-done, f32[1568,512]{1,0:T(8,128)} %copy-done.11, f32[512]{0:T(512)S(1)} %convert_element_type.168, ...), kind=kOutput, calls=%fused_computation.18 | convolution fusion | flops 3504291840 | bytes 37445888 | tf_op jit(solution)/shard_map/dot_general | solution.py:70
  552.5 16.8 %convert_reduce_fusion.1 = (f32[2048]{0:T(1024)}, bf16[1568,2048]{1,0:T(8,128)(2,1)}) fusion(f32[1568,2048]{1,0:T(8,128)} %get-tuple-element.52, bf16[1568,512]{1,0:T(8,128)(2,1)S(1)} %copy-done.18, bf16[2048,512]{1,0:T(8,128)(2,1)} %all-gather.8.cloned.1.call-done, f32[1568,2048]{1,0:T(8,128)} %get-tuple-element.66, f32[2048]{0:T(1024)S(1)} %convert_element_type.170), kind=kOutput, calls=%fused_computation.16 | convolution fusion | flops 3342923776 | bytes 35831808 | tf_op jit(solution)/shard_map/dot_general | solution.py:80
  569.3 8.1 multiply_reduce_fusion.2
  577.5 1.5 fusion.57
  579.0 1.6 convert_reduce_fusion.3
  580.6 1.1 copy-done.20
  582.9 2.4 copy.69
  585.3 6.5 reshape.403
  591.8 20.5 %fusion.16 = bf16[4,392,1,16,32]{1,4,3,0,2:T(8,128)(2,1)} fusion(f32[4,16,392,392]{2,3,1,0:T(8,128)} %get-tuple-element.63, f32[4,16,392]{2,1,0:T(8,128)S(1)} %copy-done.16, bf16[4,392,16,32]{1,0,3,2:T(4,128)(2,1)S(1)} %reshape.403), kind=kOutput, calls=%fused_computation.64 | convolution fusion | flops 649076736 | bytes 42649600 | tf_op jit(solution)/shard_map/ghqk,gqhd->gkhd/dot_general | solution.py:215
  612.2 36.0 %multiply_reduce_fusion = (f32[4,16,392]{2,1,0:T(8,128)S(1)}, f32[4,16,392,392]{2,3,1,0:T(8,128)}) fusion(f32[4,16,392,392]{2,3,1,0:T(8,128)} %get-tuple-element.63, f32[4,16,392]{2,1,0:T(8,128)S(1)} %copy-done.16, bf16[4,392,1,16,32]{1,0,4,3,2:T(4,128)(2,1)} %get-tuple-element.55, bf16[4,392,16,32]{1,0,3,2:T(4,128)(2,1)S(1)} %reshape.403), kind=kOutput, calls=%fused_computation.2 | convolution fusion | flops 658886144 | bytes 82087936 | tf_op jit(solution)/shard_map/gqhd,gkhd->ghqk/dot_general | solution.py:218
  648.3 49.6 %convert_reduce_fusion = (f32[16,392,392]{1,2,0:T(8,128)}, bf16[4,16,392,392]{2,3,1,0:T(8,128)(2,1)}) fusion(f32[4,16,392,392]{2,3,1,0:T(8,128)} %get-tuple-element.69, f32[4,16,392]{2,1,0:T(8,128)S(1)} %get-tuple-element.68, f32[4,16,392,392]{2,3,1,0:T(8,128)} %get-tuple-element.63, f32[4,16,392]{2,1,0:T(8,128)S(1)} %copy-done.16), kind=kLoop, calls=%fused_computation | loop fusion | flops 56548352 | bytes 108380160 | tf_op jit(solution)/shard_map/reduce_sum | solution.py:240
  697.9 13.8 multiply_bitcast_fusion
  711.7 46.0 %copy.76 = f32[16,392,392]{0,2,1:T(8,128)} copy(f32[16,392,392]{1,2,0:T(8,128)} %get-tuple-element.43) | data formatting | bytes 19668992 | tf_op jit(solution)/shard_map/reduce_sum | solution.py:240
  757.7 86.0 %reshape.405 = f32[16,8,7,7,8,7,7]{0,6,5,4,3,2,1:T(8,128)} reshape(f32[16,392,392]{0,2,1:T(8,128)} %copy.76) | data formatting | bytes 19668992 | tf_op jit(solution)/shard_map/reshape | solution.py:42
  843.8 49.4 %convolution_bitcast_fusion.1 = f32[16,8,7,8,7,13]{0,5,4,3,2,1:T(8,128)} fusion(f32[16,8,7,7,8,7,7]{0,6,5,4,3,2,1:T(8,128)} %reshape.405, s32[7,7]{1,0:T(8,128)S(1)} %copy-done.28), kind=kOutput, calls=%fused_computation.34 | convolution fusion | flops 383545984 | bytes 12443844 | tf_op jit(solution)/shard_map/cwe,htrcuvw->htruve/dot_general | solution.py:43
  893.2 36.4 %copy.78 = f32[16,8,7,8,7,13]{5,4,2,3,1,0:T(8,128)} copy(f32[16,8,7,8,7,13]{0,5,4,3,2,1:T(8,128)} %convolution_bitcast_fusion.1) | data formatting | bytes 5218304 | tf_op jit(solution)/shard_map/cwe,htrcuvw->htruve/dot_general | solution.py:43
  929.6 28.1 %convolution_bitcast_fusion.3 = f32[16,8,8,13,13]{3,4,2,1,0:T(8,128)} fusion(f32[16,8,7,8,7,13]{5,4,2,3,1,0:T(8,128)} %copy.78, pred[7,7,13,1,1,1]{2,1,0,5,4,3:T(8,128)(4,1)S(1)} %copy-done.47), kind=kOutput, calls=%fused_computation.59 | convolution fusion | flops 101756928 | bytes 3302013 | tf_op jit(solution)/shard_map/rvb,htruve->htube/dot_general | solution.py:44
  957.7 12.0 copy.79
  969.7 7.0 convolution_bitcast_fusion.5
  976.7 2.2 copy.80
  978.9 1.3 reshape.406
  980.7 4.1 fusion.65
  984.9 13.1 multiply_bitcast_fusion.1
  998.0 3.2 convert_reduce_fusion.2
  1001.3 8.8 copy.75
  1010.0 12.3 convert_element_type.185
  1022.3 7.8 fusion.64
  1030.4 9.0 fusion.54
  1039.5 1.3 copy-done.19
  1040.9 8.5 fusion.66
  1051.4 8.6 multiply_reduce_fusion.3
  1060.0 38.1 %all-reduce.18 = (f32[512]{0:T(512)S(1)}, f32[512]{0:T(512)S(1)}, f32[512]{0:T(512)S(1)}, f32[512]{0:T(512)S(1)}, f32[512]{0:T(512)S(1)}, /*index=5*/f32[512]{0:...) all-reduce(f32[512]{0:T(512)S(1)} %get-tuple-element.18, ...), channel_id=2, replica_groups=mesh['dp'=4,'fsdp'=8] {'dp','fsdp'}, use_global_device_ids=true, to_apply=%region_12.13.clone | all-reduce | flops 6144 | bytes 49152
  1102.8 3.7 add_add_fusion
  1106.5 2.4 reduce_sum.182
  1109.5 4.0 add_convert_fusion.3
  1114.1 7.7 multiply_convert_fusion.2
  1121.8 118.4 %reduce-scatter.7.cloned.1.call-done = f32[16,512]{1,0:T(8,128)} async-done(((f32[512,512]{1,0:T(8,128)}), f32[16,512]{1,0:T(8,128)}) %reduce-scatter.7.cloned.1.call-update) | async-done | bytes 32784 | tf_op jit(solution)/shard_map/reduce_scatter | solution.py:249
  1240.2 104.5 %reduce-scatter.5.cloned.1.call-done = f32[16,1536]{1,0:T(8,128)} async-done(((f32[512,1536]{1,0:T(8,128)}), f32[16,1536]{1,0:T(8,128)}) %reduce-scatter.5.cloned.1.call-update) | async-done | bytes 98320 | tf_op jit(solution)/shard_map/reduce_scatter | solution.py:246
  1344.7 145.4 %reduce-scatter.9.cloned.1.call-done = f32[16,2048]{1,0:T(8,128)} async-done(((f32[512,2048]{1,0:T(8,128)}), f32[16,2048]{1,0:T(8,128)}) %reduce-scatter.9.cloned.1.call-update) | async-done | bytes 131088 | tf_op jit(solution)/shard_map/reduce_scatter | solution.py:253
  1490.1 144.5 %reduce-scatter.11.cloned.1.call-done = f32[64,512]{1,0:T(8,128)} async-done(((f32[2048,512]{1,0:T(8,128)}), f32[64,512]{1,0:T(8,128)}) %reduce-scatter.11.cloned.1.call-update) | async-done | bytes 131088 | tf_op jit(solution)/shard_map/reduce_scatter | solution.py:255
  1634.6 1.6 copy.138
  (247 shorter events, 21.3 us)
Async XLA Ops:
  7.2 8.8 copy-start.74
  7.2 9.0 copy-start.75
  7.2 9.2 copy-start.76
  7.2 9.4 copy-start.77
  7.2 9.7 copy-start.78
  7.2 9.9 copy-start.79
  7.2 10.2 copy-start.80
  7.3 10.4 copy-start.81
  7.3 10.6 copy-start.82
  7.3 54.0 %copy-start.29 = (bf16[2535,16]{0,1:T(8,128)(2,1)S(1)}, bf16[2535,16]{0,1:T(8,128)(2,1)}, u32[]{:S(2)}) copy-start(bf16[2535,16]{0,1:T(8,128)(2,1)} %param.25) | copy-start | bytes 243364
  7.3 393.5 %all-gather.4.cloned.1.call-start = ((), (), s32[]{:S(2)}) async-start(), calls=%async_computation.4 | async-start | bytes 1622016 | tf_op jit(solution)/shard_map/all_gather | solution.py:121
  8.0 509.3 %all-gather.6.cloned.1.call-start = ((), (), s32[]{:S(2)}) async-start(), calls=%async_computation.5 | async-start | bytes 2162688 | tf_op jit(solution)/shard_map/all_gather | solution.py:130
  8.8 543.7 %all-gather.8.cloned.1.call-start = ((), (), s32[]{:S(2)}) async-start(), calls=%async_computation.6 | async-start | bytes 2162688 | tf_op jit(solution)/shard_map/all_gather | solution.py:132
  9.5 1112.3 %all-reduce.22.cloned.1.call-start = ((), (), s32[]{:S(2)}) async-start(), calls=%async_computation.8 | async-start | bytes 327680 | tf_op jit(solution)/shard_map/psum | solution.py:242
  9.6 56.3 %copy-start.38 = (s32[8,8]{1,0:T(8,128)}, s32[8,8]{1,0:T(8,128)S(1)}, u32[]{:S(2)}) copy-start(s32[8,8]{1,0:T(8,128)S(1)} %subtract_add_fusion.1) | copy-start | bytes 772
  9.6 68.9 %copy-start.27 = (s32[7,7]{1,0:T(8,128)}, s32[7,7]{1,0:T(8,128)S(1)}, u32[]{:S(2)}) copy-start(s32[7,7]{1,0:T(8,128)S(1)} %subtract_add_fusion) | copy-start | bytes 592
  11.4 49.3 %copy-start.22 = (f32[4,392]{1,0:T(4,128)}, f32[4,392]{1,0:T(4,128)S(1)}, u32[]{:S(2)}) copy-start(f32[4,392]{1,0:T(4,128)S(1)} %broadcast_multiply_fusion.1) | copy-start | bytes 18820
  268.3 54.6 %copy-start.69 = (bf16[512]{0:T(512)(128)(2,1)S(1)}, bf16[512]{0:T(512)(128)(2,1)}, u32[]{:S(2)}) copy-start(bf16[512]{0:T(512)(128)(2,1)} %get-tuple-element.36) | copy-start | bytes 3076
  268.3 54.6 %copy-start.68 = (bf16[512]{0:T(512)(128)(2,1)S(1)}, bf16[512]{0:T(512)(128)(2,1)}, u32[]{:S(2)}) copy-start(bf16[512]{0:T(512)(128)(2,1)} %get-tuple-element.37) | copy-start | bytes 3076
  268.3 54.7 %copy-start.40 = (f32[4,392]{1,0:T(4,128)S(1)}, f32[4,392]{1,0:T(4,128)}, u32[]{:S(2)}) copy-start(f32[4,392]{1,0:T(4,128)} %multiply_reduce_fusion.7) | copy-start | bytes 18820
  268.3 54.8 %copy-start.48 = (s32[4,3]{1,0:T(4,128)S(1)}, s32[4,3]{1,0:T(4,128)}, u32[]{:S(2)}) copy-start(s32[4,3]{1,0:T(4,128)} %param.18) | copy-start | bytes 148
  268.3 55.0 %copy-start.51 = (bf16[16,512]{1,0:T(8,128)(2,1)S(1)}, bf16[16,512]{1,0:T(8,128)(2,1)}, u32[]{:S(2)}) copy-start(bf16[16,512]{1,0:T(8,128)(2,1)} %param.26) | copy-start | bytes 49156
  268.4 128.7 %copy-start.59 = (bf16[2048]{0:T(1024)(128)(2,1)S(1)}, bf16[2048]{0:T(1024)(128)(2,1)}, u32[]{:S(2)}) copy-start(bf16[2048]{0:T(1024)(128)(2,1)} %get-tuple-element.41) | copy-start | bytes 12292
  268.4 128.7 %copy-start.67 = (bf16[512]{0:T(512)(128)(2,1)S(1)}, bf16[512]{0:T(512)(128)(2,1)}, u32[]{:S(2)}) copy-start(bf16[512]{0:T(512)(128)(2,1)} %get-tuple-element.39) | copy-start | bytes 3076
  268.4 128.7 %copy-start.66 = (bf16[512]{0:T(512)(128)(2,1)S(1)}, bf16[512]{0:T(512)(128)(2,1)}, u32[]{:S(2)}) copy-start(bf16[512]{0:T(512)(128)(2,1)} %get-tuple-element.40) | copy-start | bytes 3076
  268.4 128.8 %copy-start.54 = (s32[392]{0:T(512)S(1)}, s32[392]{0:T(512)}, u32[]{:S(2)}) copy-start(s32[392]{0:T(512)} %get-tuple-element.73) | copy-start | bytes 4708
  268.4 128.8 %copy-start.55 = (s32[392]{0:T(512)S(1)}, s32[392]{0:T(512)}, u32[]{:S(2)}) copy-start(s32[392]{0:T(512)} %get-tuple-element.74) | copy-start | bytes 4708
  268.4 128.8 %copy-start.56 = (s32[392]{0:T(512)S(1)}, s32[392]{0:T(512)}, u32[]{:S(2)}) copy-start(s32[392]{0:T(512)} %add_select_fusion.4) | copy-start | bytes 4708
  268.4 128.9 %copy-start.4 = (bf16[4,392,512]{2,1,0:T(8,128)(2,1)S(1)}, bf16[4,392,512]{2,1,0:T(8,128)(2,1)}, u32[]{:S(2)}) copy-start(bf16[4,392,512]{2,1,0:T(8,128)(2,1)} %param.19) | copy-start | bytes 4816900
  322.9 76.0 %copy-start.70 = (bf16[512]{0:T(512)(128)(2,1)S(1)}, bf16[512]{0:T(512)(128)(2,1)}, u32[]{:S(2)}) copy-start(bf16[512]{0:T(512)(128)(2,1)} %get-tuple-element.34) | copy-start | bytes 3076
  322.9 76.0 %copy-start.71 = (bf16[512]{0:T(512)(128)(2,1)S(1)}, bf16[512]{0:T(512)(128)(2,1)}, u32[]{:S(2)}) copy-start(bf16[512]{0:T(512)(128)(2,1)} %get-tuple-element.35) | copy-start | bytes 3076
  322.9 76.0 %copy-start.2 = (bf16[4,392,512]{2,1,0:T(8,128)(2,1)S(1)}, bf16[4,392,512]{2,1,0:T(8,128)(2,1)}, u32[]{:S(2)}) copy-start(bf16[4,392,512]{2,1,0:T(8,128)(2,1)} %param.17) | copy-start | bytes 4816900
  322.9 76.0 %copy-start.23 = (f32[4,392]{1,0:T(4,128)S(1)}, f32[4,392]{1,0:T(4,128)}, u32[]{:S(2)}) copy-start(f32[4,392]{1,0:T(4,128)} %copy-done.22) | copy-start | bytes 18820
  323.0 77.8 %copy-start.49 = (f32[512]{0:T(512)}, f32[512]{0:T(512)S(1)}, u32[]{:S(2)}) copy-start(f32[512]{0:T(512)S(1)} %convert_element_type.156) | copy-start | bytes 6148
  323.1 74.2 %copy-start.32 = (f32[1568]{0:T(1024)}, f32[1568]{0:T(1024)S(1)}, u32[]{:S(2)}) copy-start(f32[1568]{0:T(1024)S(1)} %add.190) | copy-start | bytes 18820
  323.1 77.6 %copy-start.43 = (f32[1568]{0:T(1024)}, f32[1568]{0:T(1024)S(1)}, u32[]{:S(2)}) copy-start(f32[1568]{0:T(1024)S(1)} %rsqrt.23) | copy-start | bytes 18820
  397.1 120.2 %copy-start.62 = (f32[512]{0:T(512)}, f32[512]{0:T(512)S(1)}, u32[]{:S(2)}) copy-start(f32[512]{0:T(512)S(1)} %convert_element_type.168) | copy-start | bytes 6148
  397.1 180.3 %copy-start.57 = (f32[512]{0:T(512)}, f32[512]{0:T(512)S(1)}, u32[]{:S(2)}) copy-start(f32[512]{0:T(512)S(1)} %convert_element_type.167) | copy-start | bytes 6148
  438.4 29.8 %copy-start.7 = (bf16[4,392,1,16,32]{1,0,4,3,2:T(4,128)(2,1)}, bf16[4,392,1,16,32]{1,0,4,3,2:T(4,128)(2,1)S(1)}, u32[]{:S(2)}) copy-start(bf16[4,392,1,16,32]{1,0,4,3,2:T(4,128)(2,1)S(1)} %get-tuple-element.57) | copy-start | bytes 4816900
  438.4 29.8 %copy-start.9 = (bf16[4,392,1,16,32]{1,0,4,3,2:T(4,128)(2,1)}, bf16[4,392,1,16,32]{1,0,4,3,2:T(4,128)(2,1)S(1)}, u32[]{:S(2)}) copy-start(bf16[4,392,1,16,32]{1,0,4,3,2:T(4,128)(2,1)S(1)} %get-tuple-element.56) | copy-start | bytes 4816900
  514.8 62.6 %copy-start.36 = (f32[1568]{0:T(1024)}, f32[1568]{0:T(1024)S(1)}, u32[]{:S(2)}) copy-start(f32[1568]{0:T(1024)S(1)} %broadcast_multiply_fusion) | copy-start | bytes 18820
  517.3 60.2 %copy-start.45 = (f32[1568]{0:T(1024)}, f32[1568]{0:T(1024)S(1)}, u32[]{:S(2)}) copy-start(f32[1568]{0:T(1024)S(1)} %fusion.45) | copy-start | bytes 18820
  517.3 35.2 %copy-start.18 = (bf16[1568,512]{1,0:T(8,128)(2,1)S(1)}, bf16[1568,512]{1,0:T(8,128)(2,1)}, u32[]{:S(2)}) copy-start(bf16[1568,512]{1,0:T(8,128)(2,1)} %fusion.15) | copy-start | bytes 4816900
  552.5 16.9 %copy-start.12 = (f32[1568,512]{1,0:T(8,128)S(1)}, f32[1568,512]{1,0:T(8,128)}, u32[]{:S(2)}) copy-start(f32[1568,512]{1,0:T(8,128)} %copy-done.11) | copy-start | bytes 9633796
  552.5 16.9 %copy-start.73 = (bf16[512,2048]{1,0:T(8,128)(2,1)S(1)}, bf16[512,2048]{1,0:T(8,128)(2,1)}, u32[]{:S(2)}) copy-start(bf16[512,2048]{1,0:T(8,128)(2,1)} %all-gather.6.cloned.1.call-done) | copy-start | bytes 6291460
  582.9 8.9 copy-start.16
  648.3 49.6 %copy-start.10 = (bf16[4,392,1,16,32]{1,0,4,3,2:T(4,128)(2,1)S(1)}, bf16[4,392,1,16,32]{1,0,4,3,2:T(4,128)(2,1)}, u32[]{:S(2)}) copy-start(bf16[4,392,1,16,32]{1,0,4,3,2:T(4,128)(2,1)} %copy-done.9) | copy-start | bytes 4816900
  757.7 86.0 %copy-start.28 = (s32[7,7]{1,0:T(8,128)S(1)}, s32[7,7]{1,0:T(8,128)}, u32[]{:S(2)}) copy-start(s32[7,7]{1,0:T(8,128)} %copy-done.27) | copy-start | bytes 592
  893.2 36.5 %copy-start.47 = (pred[7,7,13,1,1,1]{2,1,0,5,4,3:T(8,128)(4,1)S(1)}, pred[7,7,13,1,1,1]{2,1,0,5,4,3:T(8,128)(4,1)}, u32[]{:S(2)}) copy-start(pred[7,7,13,1,1,1]{2,1,0,5,4,3:T(8,128)(4,1)} %fusion.96) | copy-start | bytes 1915
  957.7 12.0 copy-start.39
  980.2 259.9 %reduce-scatter.7.cloned.1.call-start = ((), (), s32[]{:S(2)}) async-start(), calls=%async_computation.9 | async-start | bytes 1081344 | tf_op jit(solution)/shard_map/reduce_scatter | solution.py:249
  984.9 359.8 %reduce-scatter.5.cloned.1.call-start = ((), (), s32[]{:S(2)}) async-start(), calls=%async_computation.7 | async-start | bytes 3244032 | tf_op jit(solution)/shard_map/reduce_scatter | solution.py:246
  984.9 13.1 copy-start.15
  1022.3 8.1 copy-start.37
  1022.3 8.1 copy-start.46
  1022.3 8.1 copy-start.58
  1022.3 8.1 copy-start.63
  1030.2 459.9 %reduce-scatter.9.cloned.1.call-start = ((), (), s32[]{:S(2)}) async-start(), calls=%async_computation.10 | async-start | bytes 4325376 | tf_op jit(solution)/shard_map/reduce_scatter | solution.py:253
  1039.5 595.1 %reduce-scatter.11.cloned.1.call-start = ((), (), s32[]{:S(2)}) async-start(), calls=%async_computation.11 | async-start | bytes 4325376 | tf_op jit(solution)/shard_map/reduce_scatter | solution.py:255
  1051.3 8.7 copy-start.52
  1051.4 8.7 copy-start.53
  1051.4 8.7 copy-start.60
  1051.4 8.7 copy-start.61
  1051.4 51.4 %copy-start.33 = (f32[1568]{0:T(1024)S(1)}, f32[1568]{0:T(1024)}, u32[]{:S(2)}) copy-start(f32[1568]{0:T(1024)} %copy-done.32) | copy-start | bytes 18820
  (27 other events, 75.3 us)
Sparse Core Ops, SparseCore 0:
  11.1 58.1 all-gather.3
  72.2 55.3 all-gather.5
  130.7 55.3 all-gather.7
  980.3 119.7 all-reduce.21
  1102.8 137.3 reduce-scatter.6
  1246.9 97.7 reduce-scatter.4
  1347.6 142.4 reduce-scatter.8
  1493.0 141.4 reduce-scatter.10
where the time goes:
time: 1650 us; the launch traced here: 1640 us
  waiting for transfers between devices  515 us (31%)
  local copies, waits for them, and re-layouts  471 us (29%)
  matrix products  392 us (24%)
  blocking collectives  154 us (9%)
  other arithmetic  94.8 us (6%)
    reduce_scatter x1, waiting for transfers between devices, per_device(): lax.psum_scatter(fc1_grad, ('dp', 'fsdp'), scatter_dimension=0, tiled=True)  145 us
    reduce_scatter x1, waiting for transfers between devices, per_device(): lax.psum_scatter(fc2_grad, ('dp', 'fsdp'), scatter_dimension=0, tiled=True)  144 us
    add x2, local copies, waits for them, and re-layouts, attention_scores(): scores = scores + bias[None]  140 us
    reduce_scatter x1, waiting for transfers between devices, per_device(): lax.psum_scatter(proj_grad, ('dp', 'fsdp'), scatter_dimension=0, tiled=True)  118 us
    reduce_scatter x1, waiting for transfers between devices, per_device(): lax.psum_scatter(qkv_weight_grad, ('dp', 'fsdp'), scatter_dimension=0, ti...  105 us
    reshape x1, local copies, waits for them, and re-layouts, fold_bias(): spread = bias_grad.reshape(HEADS, WIN_T, WIN_H, WIN_W, WIN_T, WIN_H, WIN_W)  86 us
    unnamed x2, blocking collectives  80.6 us
    all_gather x1, blocking collectives, per_device(): lax.all_gather(proj_weight, ('dp', 'fsdp'), axis=0, tiled=True)  73.8 us
  transfers between devices with their start and end apart: 8, of which 4 were waited for; matrix products, arithmetic and copies ran while one was open for 32% of the time, Pallas kernels for 0%

commit v1 on v0

v1 whole, which is shorter than its diff:
```python
import functools
import math

import jax
import jax.numpy as jnp
import numpy as np
from jax import lax
from jax.experimental import pallas as pl
from jax.experimental.pallas import tpu as pltpu
from jax.sharding import PartitionSpec as P

D = 512
HEADS = 16
HDIM = 32
FF = 2048
WIN_T = 8
WIN_H = 7
WIN_W = 7
WIN = WIN_T * WIN_H * WIN_W
FLAT = WIN_H * WIN_W
OFFS_T = 2 * WIN_T - 1
OFFS_H = 2 * WIN_H - 1
OFFS_W = 2 * WIN_W - 1
SPREAD = OFFS_T * FLAT
EPS = 1e-05
LOG2E = math.log2(math.e)
LN2 = math.log(2.0)
SCALE = HDIM ** (-0.5)
AXES = ("dp", "fsdp")
BF16 = jnp.bfloat16
F32 = jnp.float32
MIB = 2**20


def dot(left, right, left_dim, right_dim):
    return lax.dot_general(
        left, right, (((left_dim,), (right_dim,)), ((), ())), preferred_element_type=F32
    )


def dot_nn(left, right):
    return dot(left, right, 1, 0)


def dot_nt(left, right):
    return dot(left, right, 1, 1)


def dot_tn(left, right):
    return dot(left, right, 0, 0)


def standardize(rows):
    average = jnp.mean(rows, axis=-1, keepdims=True)
    centered = rows - average
    variance = jnp.mean(centered * centered, axis=-1, keepdims=True)
    scale = lax.rsqrt(variance + EPS)
    return centered * scale, scale


def norm_backward(grad, unit, scale, gain):
    scaled = grad * gain
    first = jnp.mean(scaled, axis=-1, keepdims=True)
    second = jnp.mean(scaled * unit, axis=-1, keepdims=True)
    return (scaled - first - unit * second) * scale


def gelu_parts(hidden):
    reach = jnp.abs(hidden) * (0.5**0.5)
    ratio = 1.0 / (1.0 + 0.3275911 * reach)
    series = 1.061405429 * ratio - 1.453152027
    series = series * ratio + 1.421413741
    series = series * ratio - 0.284496736
    series = series * ratio + 0.254829592
    bell = jnp.exp(-0.5 * hidden * hidden)
    tail = (0.5 * series) * (ratio * bell)
    below = jnp.where(hidden < 0, tail, 1.0 - tail)
    return hidden * below, below + hidden * bell * (1.0 / math.sqrt(2 * math.pi))


def qkv_kernel(x_ref, gain_ref, shift_ref, weight_ref, bias_ref, out_ref):
    unit, _ = standardize(x_ref[...].astype(F32))
    normed = (unit * gain_ref[...] + shift_ref[...]).astype(BF16)
    for part in range(3):
        columns = slice(part * D, (part + 1) * D)
        got = dot_nn(normed, weight_ref[:, columns]) + bias_ref[:, columns]
        if part == 0:
            got = got * (SCALE * LOG2E)
        out_ref[:, columns] = got.astype(BF16)


def project_qkv(x_rows, gain, shift, weight, bias):
    rows = x_rows.shape[0]
    block = rows // 2
    whole = lambda i: (0, 0)
    return pl.pallas_call(
        qkv_kernel,
        grid=(2,),
        in_specs=[
            pl.BlockSpec((block, D), lambda i: (i, 0)),
            pl.BlockSpec((1, D), whole),
            pl.BlockSpec((1, D), whole),
            pl.BlockSpec((D, 3 * D), whole),
            pl.BlockSpec((1, 3 * D), whole),
        ],
        out_specs=pl.BlockSpec((block, 3 * D), lambda i: (i, 0)),
        out_shape=jax.ShapeDtypeStruct((rows, 3 * D), BF16),
        compiler_params=pltpu.CompilerParams(vmem_limit_bytes=48 * MIB),
        name="norm_qkv",
    )(x_rows, gain, shift, weight, bias)


def attend_kernel(
    windows, qkv_ref, spread_ref, keyrow_ref, qkvt_ref, probs_ref, att_ref, attt_ref, inv_ref, bias_ref
):
    head = pl.program_id(0)

    @pl.when(head == 0)
    def _():
        for w in range(windows):
            for part in range(12):
                rows = slice(part * 128, (part + 1) * 128)
                qkvt_ref[w, rows, :] = qkv_ref[w, :, rows].astype(F32).T.astype(BF16)

    for u in range(WIN_T):
        start = (WIN_T - 1 - u) * FLAT
        bias_ref[u * FLAT : (u + 1) * FLAT, :] = spread_ref[0, :, start : start + WIN]
    row = pl.multiple_of(head * HDIM, HDIM)
    ones = jnp.ones((16, WIN), BF16)
    for w in range(windows):
        queries = qkvt_ref[w, pl.ds(row, HDIM), :]
        keys = qkvt_ref[w, pl.ds(row + D, HDIM), :]
        values = qkvt_ref[w, pl.ds(row + 2 * D, HDIM), :]
        scores = dot_tn(
            jnp.concatenate([keys, keyrow_ref[w]], axis=0), jnp.concatenate([queries, ones], axis=0)
        )
        scores = scores + bias_ref[...]
        top = jnp.max(scores, axis=0, keepdims=True)
        expo = jnp.exp2(scores - top).astype(BF16)
        probs_ref[w, 0] = expo
        mixed = dot_nn(jnp.concatenate([values, ones], axis=0), expo)
        inverse = 1.0 / mixed[HDIM : HDIM + 1]
        inv_ref[w, pl.ds(head, 1), :] = inverse
        attt_ref[w, pl.ds(row, HDIM), :] = (mixed[:HDIM] * inverse).astype(BF16)

    @pl.when(head == HEADS - 1)
    def _():
        for w in range(windows):
            for part in range(4):
                rows = slice(part * 128, (part + 1) * 128)
                att_ref[w, :, rows] = attt_ref[w, rows, :].astype(F32).T.astype(BF16)


def attend(qkv, spread, keyrow):
    windows = qkv.shape[0]
    whole = lambda h: (0, 0, 0)
    return pl.pallas_call(
        functools.partial(attend_kernel, windows),
        grid=(HEADS,),
        in_specs=[
            pl.BlockSpec((windows, WIN, 3 * D), whole),
            pl.BlockSpec((1, FLAT, SPREAD), lambda h: (h, 0, 0)),
            pl.BlockSpec((windows, 16, WIN), whole),
        ],
        out_specs=[
            pl.BlockSpec((windows, 3 * D, WIN), whole),
            pl.BlockSpec((windows, 1, WIN, WIN), lambda h: (0, h, 0, 0)),
            pl.BlockSpec((windows, WIN, D), whole),
            pl.BlockSpec((windows, D, WIN), whole),
            pl.BlockSpec((windows, HEADS, WIN), whole),
        ],
        out_shape=[
            jax.ShapeDtypeStruct((windows, 3 * D, WIN), BF16),
            jax.ShapeDtypeStruct((windows, HEADS, WIN, WIN), BF16),
            jax.ShapeDtypeStruct((windows, WIN, D), BF16),
            jax.ShapeDtypeStruct((windows, D, WIN), BF16),
            jax.ShapeDtypeStruct((windows, HEADS, WIN), F32),
        ],
        scratch_shapes=[pltpu.VMEM((WIN, WIN), F32)],
        compiler_params=pltpu.CompilerParams(vmem_limit_bytes=60 * MIB),
        name="attend",
    )(qkv, spread, keyrow)


def mlp_kernel(
    x_ref,
    att_ref,
    cot_ref,
    keep_ref,
    proj_ref,
    pshift_ref,
    gain_ref,
    shift_ref,
    fc1_ref,
    fshift1_ref,
    fc2_ref,
    fshift2_ref,
    out_ref,
    rgrad_ref,
    agrad_ref,
    fc1g_ref,
    fc2g_ref,
    projg_ref,
    sums_ref,
    fsum_ref,
    act_ref,
    hid_ref,
    norm_ref,
    gout_ref,
    branch_ref,
):
    rows = x_ref.shape[0]
    block = rows // 2
    pieces = 4
    wide = FF // pieces
    sums_ref[...] = jnp.zeros_like(sums_ref)
    fsum_ref[...] = jnp.zeros_like(fsum_ref)

    def one_block(i, carry):
        at = pl.ds(pl.multiple_of(i * block, 16), block)
        keep = keep_ref[at, :]
        resid = x_ref[at, :].astype(F32) + dot_nn(att_ref[at, :], proj_ref[...]) + pshift_ref[...]
        unit, scale = standardize(resid)
        normed = (unit * gain_ref[...] + shift_ref[...]).astype(BF16)
        norm_ref[at, :] = normed
        gout = cot_ref[at, :].astype(F32) * keep
        gout_low = gout.astype(BF16)
        gout_ref[at, :] = gout_low
        total = resid + fshift2_ref[...]
        grad_two = None
        for part in range(pieces):
            columns = slice(part * wide, (part + 1) * wide)
            hidden = dot_nn(normed, fc1_ref[:, columns]) + fshift1_ref[:, columns]
            active, slope = gelu_parts(hidden)
            active = active.astype(BF16)
            act_ref[at, columns] = active
            total = total + dot_nn(active, fc2_ref[columns, :])
            hgrad = (dot_nt(gout_low, fc2_ref[columns, :]) * slope).astype(BF16)
            hid_ref[at, columns] = hgrad
            fsum_ref[0:1, columns] += jnp.sum(hgrad.astype(F32), axis=0, keepdims=True)
            back = dot_nt(hgrad, fc1_ref[:, columns])
            grad_two = back if grad_two is None else grad_two + back
        out_ref[at, :] = (total * keep).astype(BF16)
        rgrad = gout + norm_backward(grad_two, unit, scale, gain_ref[...])
        rgrad_ref[at, :] = rgrad
        branch = rgrad.astype(BF16)
        branch_ref[at, :] = branch
        agrad_ref[at, :] = dot_nt(branch, proj_ref[...]).astype(BF16)
        sums_ref[0:1, :] += jnp.sum(gout, axis=0, keepdims=True)
        sums_ref[1:2, :] += jnp.sum(grad_two * unit, axis=0, keepdims=True)
        sums_ref[2:3, :] += jnp.sum(grad_two, axis=0, keepdims=True)
        sums_ref[3:4, :] += jnp.sum(branch.astype(F32), axis=0, keepdims=True)
        return carry

    lax.fori_loop(0, 2, one_block, 0)
    projg_ref[...] = dot_tn(att_ref[...], branch_ref[...])
    for part in range(pieces):
        columns = slice(part * wide, (part + 1) * wide)
        fc2g_ref[columns, :] = dot_tn(act_ref[:, columns], gout_ref[...])
        fc1g_ref[:, columns] = dot_tn(norm_ref[...], hid_ref[:, columns])


def feed_forward(x_rows, att_rows, cot_rows, keep_rows, proj, pshift, gain, shift, fc1, fshift1, fc2, fshift2):
    rows = x_rows.shape[0]
    vmem = pl.BlockSpec(memory_space=pltpu.VMEM)
    return pl.pallas_call(
        mlp_kernel,
        in_specs=[vmem] * 12,
        out_specs=[vmem] * 8,
        out_shape=[
            jax.ShapeDtypeStruct((rows, D), BF16),
            jax.ShapeDtypeStruct((rows, D), F32),
            jax.ShapeDtypeStruct((rows, D), BF16),
            jax.ShapeDtypeStruct((D, FF), F32),
            jax.ShapeDtypeStruct((FF, D), F32),
            jax.ShapeDtypeStruct((D, D), F32),
            jax.ShapeDtypeStruct((8, D), F32),
            jax.ShapeDtypeStruct((8, FF), F32),
        ],
        scratch_shapes=[
            pltpu.VMEM((rows, FF), BF16),
            pltpu.VMEM((rows, FF), BF16),
            pltpu.VMEM((rows, D), BF16),
            pltpu.VMEM((rows, D), BF16),
            pltpu.VMEM((rows, D), BF16),
        ],
        compiler_params=pltpu.CompilerParams(vmem_limit_bytes=62 * MIB),
        name="feed_forward",
    )(x_rows, att_rows, cot_rows, keep_rows, proj, pshift, gain, shift, fc1, fshift1, fc2, fshift2)


def attend_back_kernel(
    windows,
    qkvt_ref,
    attt_ref,
    agrad_ref,
    inv_ref,
    probs_ref,
    dqkv_ref,
    fold_ref,
    dot_ref,
    dqkvt_ref,
    sum_ref,
    wide_ref,
):
    head = pl.program_id(0)

    @pl.when(head == 0)
    def _():
        for w in range(windows):
            for part in range(4):
                rows = slice(part * 128, (part + 1) * 128)
                dot_ref[w, rows, :] = agrad_ref[w, :, rows].astype(F32).T.astype(BF16)

    row = pl.multiple_of(head * HDIM, HDIM)
    ones = jnp.ones((16, WIN), BF16)
    place = lax.broadcasted_iota(jnp.int32, (16, WIN), 0)
    for w in range(windows):
        queries = qkvt_ref[w, pl.ds(row, HDIM), :]
        keys = qkvt_ref[w, pl.ds(row + D, HDIM), :]
        values = qkvt_ref[w, pl.ds(row + 2 * D, HDIM), :]
        expo = probs_ref[w, 0]
        grad = dot_ref[w, pl.ds(row, HDIM), :].astype(F32) * inv_ref[w, pl.ds(head, 1), :]
        inner = -jnp.sum(grad * attt_ref[w, pl.ds(row, HDIM), :].astype(F32), axis=0, keepdims=True)
        high = inner.astype(BF16).astype(F32)
        middle = (inner - high).astype(BF16).astype(F32)
        lowest = inner - high - middle
        extra = jnp.where(
            place == 0, high, jnp.where(place == 1, middle, jnp.where(place == 2, lowest, 0.0))
        ).astype(BF16)
        grad = grad.astype(BF16)
        probs_grad = dot_tn(
            jnp.concatenate([values, ones], axis=0), jnp.concatenate([grad, extra], axis=0)
        )
        scores_grad = expo.astype(F32) * probs_grad
        low = scores_grad.astype(BF16)
        if w == 0:
            sum_ref[...] = scores_grad
        else:
            sum_ref[...] += scores_grad
        dqkvt_ref[w, pl.ds(row, HDIM), :] = (dot_nn(keys, low) * SCALE).astype(BF16)
        dqkvt_ref[w, pl.ds(row + D, HDIM), :] = (dot_nt(queries, low) * LN2).astype(BF16)
        dqkvt_ref[w, pl.ds(row + 2 * D, HDIM), :] = dot_nt(grad, expo).astype(BF16)

    wide_ref[...] = jnp.zeros_like(wide_ref)
    for u in range(WIN_T):
        start = (WIN_T - 1 - u) * FLAT
        wide_ref[:, start : start + WIN] += sum_ref[u * FLAT : (u + 1) * FLAT, :]
    fold_ref[0] = wide_ref[...]

    @pl.when(head == HEADS - 1)
    def _():
        for w in range(windows):
            for part in range(12):
                rows = slice(part * 128, (part + 1) * 128)
                dqkv_ref[w, :, rows] = dqkvt_ref[w, rows, :].astype(F32).T.astype(BF16)


def attend_back(qkvt, attt, agrad, inverse, probs):
    windows = qkvt.shape[0]
    whole = lambda h: (0, 0, 0)
    return pl.pallas_call(
        functools.partial(attend_back_kernel, windows),
        grid=(HEADS,),
        in_specs=[
            pl.BlockSpec((windows, 3 * D, WIN), whole, pipeline_mode=pl.Buffered(1)),
            pl.BlockSpec((windows, D, WIN), whole, pipeline_mode=pl.Buffered(1)),
            pl.BlockSpec((windows, WIN, D), whole, pipeline_mode=pl.Buffered(1)),
            pl.BlockSpec((windows, HEADS, WIN), whole),
            pl.BlockSpec((windows, 1, WIN, WIN), lambda h: (0, h, 0, 0)),
        ],
        out_specs=[
            pl.BlockSpec((windows, WIN, 3 * D), whole),
            pl.BlockSpec((1, FLAT, SPREAD), lambda h: (h, 0, 0)),
        ],
        out_shape=[
            jax.ShapeDtypeStruct((windows, WIN, 3 * D), BF16),
            jax.ShapeDtypeStruct((HEADS, FLAT, SPREAD), F32),
        ],
        scratch_shapes=[
            pltpu.VMEM((windows, D, WIN), BF16),
            pltpu.VMEM((windows, 3 * D, WIN), BF16),
            pltpu.VMEM((WIN, WIN), F32),
            pltpu.VMEM((FLAT, SPREAD), F32),
        ],
        compiler_params=pltpu.CompilerParams(vmem_limit_bytes=62 * MIB),
        name="attend_back",
    )(qkvt, attt, agrad, inverse, probs)


def qkv_back_kernel(
    x_ref, dqkv_ref, rgrad_ref, gain_ref, shift_ref, weight_ref, igrad_ref, wgrad_ref, sums_ref, norm_ref
):
    rows = x_ref.shape[0]
    block = rows // 2
    sums_ref[...] = jnp.zeros_like(sums_ref)

    def one_block(i, carry):
        at = pl.ds(pl.multiple_of(i * block, 16), block)
        unit, scale = standardize(x_ref[at, :].astype(F32))
        norm_ref[at, :] = (unit * gain_ref[...] + shift_ref[...]).astype(BF16)
        back = dot_nt(dqkv_ref[at, :], weight_ref[...])
        igrad_ref[at, :] = (rgrad_ref[at, :] + norm_backward(back, unit, scale, gain_ref[...])).astype(BF16)
        sums_ref[0:1, :D] += jnp.sum(back * unit, axis=0, keepdims=True)
        sums_ref[1:2, :D] += jnp.sum(back, axis=0, keepdims=True)
        sums_ref[2:3, :] += jnp.sum(dqkv_ref[at, :].astype(F32), axis=0, keepdims=True)
        return carry

    lax.fori_loop(0, 2, one_block, 0)
    for part in range(3):
        columns = slice(part * D, (part + 1) * D)
        wgrad_ref[:, columns] = dot_tn(norm_ref[...], dqkv_ref[:, columns])


def qkv_back(x_rows, dqkv_rows, rgrad, gain, shift, weight):
    rows = x_rows.shape[0]
    vmem = pl.BlockSpec(memory_space=pltpu.VMEM)
    return pl.pallas_call(
        qkv_back_kernel,
        in_specs=[vmem] * 6,
        out_specs=[vmem] * 3,
        out_shape=[
            jax.ShapeDtypeStruct((rows, D), BF16),
            jax.ShapeDtypeStruct((D, 3 * D), F32),
            jax.ShapeDtypeStruct((8, 3 * D), F32),
        ],
        scratch_shapes=[pltpu.VMEM((rows, D), BF16)],
        compiler_params=pltpu.CompilerParams(vmem_limit_bytes=62 * MIB),
        name="qkv_back",
    )(x_rows, dqkv_rows, rgrad, gain, shift, weight)


def offset_choice():
    spots = np.arange(FLAT)
    rows, columns = spots // WIN_W, spots % WIN_W
    index = (rows[None, :] - rows[:, None] + WIN_H - 1) * OFFS_W + (
        columns[None, :] - columns[:, None] + WIN_W - 1
    )
    return jnp.asarray(index.reshape(1, -1)) == jnp.arange(OFFS_H * OFFS_W)[:, None]


def spread_table(bias_table):
    table = bias_table.reshape(OFFS_T, OFFS_H * OFFS_W, HEADS)
    table = jnp.transpose(table, (2, 0, 1)).reshape(HEADS * OFFS_T, OFFS_H * OFFS_W)
    wide = dot_nn(table, offset_choice().astype(BF16)) * LOG2E
    wide = wide.reshape(HEADS, OFFS_T, FLAT, FLAT)
    return jnp.transpose(wide, (0, 2, 1, 3)).reshape(HEADS, FLAT, SPREAD)


def fold_table(spread_grad):
    wide = spread_grad.reshape(HEADS, FLAT, OFFS_T, FLAT)
    wide = jnp.transpose(wide, (0, 2, 1, 3)).reshape(HEADS * OFFS_T, FLAT * FLAT)
    table = lax.dot_general(
        wide,
        offset_choice().astype(F32),
        (((1,), (1,)), ((), ())),
        precision=lax.Precision.HIGHEST,
        preferred_element_type=F32,
    )
    table = table.reshape(HEADS, OFFS_T, OFFS_H * OFFS_W)
    return jnp.transpose(table, (1, 2, 0)).reshape(-1, HEADS)


def valid_mask(extents):
    spots = np.arange(WIN)
    depth, height, across = spots // FLAT, spots // WIN_W % WIN_H, spots % WIN_W
    return (
        (depth[None, :] < extents[:, 0:1])
        & (height[None, :] < extents[:, 1:2])
        & (across[None, :] < extents[:, 2:3])
    ).astype(F32)


def gathered(value):
    return lax.all_gather(value, AXES, axis=0, tiled=True)


def scattered(value):
    return lax.psum_scatter(value, AXES, scatter_dimension=0, tiled=True)


def per_device(
    inputs,
    extents,
    cotangent,
    ln1_gain,
    ln1_shift,
    qkv_weight,
    query_bias,
    value_bias,
    bias_table,
    proj_weight,
    proj_shift,
    ln2_gain,
    ln2_shift,
    fc1_weight,
    fc1_shift,
    fc2_weight,
    fc2_shift,
):
    windows = inputs.shape[0]
    rows = windows * WIN
    qkv_full = gathered(qkv_weight)
    proj_full = gathered(proj_weight)
    fc1_full = gathered(fc1_weight)
    fc2_full = gathered(fc2_weight)
    shards = (
        ln1_gain,
        ln1_shift,
        query_bias,
        value_bias,
        proj_shift,
        ln2_gain,
        ln2_shift,
        fc2_shift,
    )
    small = ln1_gain.shape[0]
    packed = lax.all_gather(jnp.concatenate(shards + (fc1_shift,)), AXES, axis=0)
    vectors = [
        packed[:, i * small : (i + 1) * small].reshape(1, D).astype(F32) for i in range(len(shards))
    ]
    gain1, shift1, qbias, vbias, pshift, gain2, shift2, fshift2 = vectors
    fshift1 = packed[:, len(shards) * small :].reshape(1, FF).astype(F32)
    qkv_bias = jnp.concatenate([qbias, jnp.zeros_like(qbias), vbias], axis=1)

    keep = valid_mask(extents)
    keep_rows = keep.reshape(rows, 1)
    keyrow = jnp.concatenate(
        [((keep - 1.0) * 1e30)[:, None, :], jnp.zeros((windows, 15, WIN), F32)], axis=1
    ).astype(BF16)
    spread = spread_table(bias_table)

    x_rows = inputs.reshape(rows, D)
    qkv = project_qkv(x_rows, gain1, shift1, qkv_full, qkv_bias)
    qkvt, probs, att, attt, inverse = attend(qkv.reshape(windows, WIN, 3 * D), spread, keyrow)
    output, rgrad, agrad, fc1_grad, fc2_grad, proj_grad, sums, fsum = feed_forward(
        x_rows,
        att.reshape(rows, D),
        cotangent.reshape(rows, D),
        keep_rows,
        proj_full,
        pshift,
        gain2,
        shift2,
        fc1_full,
        fshift1,
        fc2_full,
        fshift2,
    )
    dqkv, spread_grad = attend_back(qkvt, attt, agrad.reshape(windows, WIN, D), inverse, probs)
    input_grad, qkv_grad, qsums = qkv_back(
        x_rows, dqkv.reshape(rows, 3 * D), rgrad, gain1, shift1, qkv_full
    )
    table_grad = lax.psum(fold_table(spread_grad), AXES)
    count = D // small
    vector_grads = jnp.concatenate(
        [
            item.reshape(count, -1)
            for item in (
                qsums[0, :D],
                qsums[1, :D],
                qsums[2, :D],
                qsums[2, 2 * D :],
                sums[3],
                sums[1],
                sums[2],
                sums[0],
                fsum[0],
            )
        ],
        axis=1,
    )
    vector_grads = scattered(vector_grads).reshape(-1)
    owned = [vector_grads[i * small : (i + 1) * small] for i in range(8)]
    return (
        output.reshape(inputs.shape),
        input_grad.reshape(inputs.shape),
        owned[0],
        owned[1],
        scattered(qkv_grad),
        owned[2],
        owned[3],
        table_grad,
        scattered(proj_grad),
        owned[4],
        owned[5],
        owned[6],
        scattered(fc1_grad),
        vector_grads[8 * small :],
        scattered(fc2_grad),
        owned[7],
    )


def solution(mesh):
    rows = P(AXES, None)
    vector = P(AXES)
    block = P(AXES, None, None)
    in_specs = (
        block,
        rows,
        block,
        vector,
        vector,
        rows,
        vector,
        vector,
        P(),
        rows,
        vector,
        vector,
        vector,
        rows,
        vector,
        rows,
        vector,
    )
    out_specs = (
        block,
        block,
        vector,
        vector,
        rows,
        vector,
        vector,
        P(),
        rows,
        vector,
        vector,
        vector,
        rows,
        vector,
        rows,
        vector,
    )
    return jax.shard_map(
        per_device, mesh=mesh, in_specs=in_specs, out_specs=out_specs, check_vma=False
    )
```

time: 1650 us -> 989 us (0.60)
  local copies, waits for them, and re-layouts: 471 us -> 63.3 us
  matrix products: 392 us -> 2.72 us
  Pallas kernels: 0 us -> 143 us
  other arithmetic: 94.8 us -> 0.99 us
  waiting for transfers between devices: 515 us -> 601 us
    dot_general x24 -> x2, matrix products: 392 us -> 2.72 us  [the longest x1 1.46 us: fold_table(): lax.dot_general(wide, offset_choice().astype(F32), (((1,), (1,)), ((), ()...]
    pallas_call x0 -> x5, Pallas kernels: none -> 143 us  [the longest x1 44.3 us: attend_back(): pl.pallas_call(functools.partial(attend_back_kernel, windows), grid=(HEAD...]
    add x3 -> x0, local copies, waits for them, and re-layouts: 140 us -> none  [the longest x2 140 us: attention_scores(): scores = scores + bias[None]]
    reduce_sum x10 -> x0, other arithmetic: 80.6 us -> none  [the longest x1 49.6 us: per_device(): bias_grad = jnp.sum(scores_grad.astype(jnp.float32), axis=0)]
    reshape x5 -> x7, local copies, waits for them, and re-layouts: 96.8 us -> 26.6 us  [the longest x2 13.4 us: spread_table(): return jnp.transpose(wide, (0, 2, 1, 3)).reshape(HEADS, FLAT, SPREAD)]
    transpose x3 -> x2, local copies, waits for them, and re-layouts: 73.5 us -> 9.31 us  [the longest x1 9.17 us: fold_table(): jnp.transpose(wide, (0, 2, 1, 3)).reshape(HEADS * OFFS_T, FLAT * FLAT)]
    psum x1, waiting for transfers between devices: 0.01 us -> 62 us  [per_device(): table_grad = lax.psum(fold_table(spread_grad), AXES)]
    reduce_sum x1 -> x0, local copies, waits for them, and re-layouts: 46 us -> none  [per_device(): bias_grad = jnp.sum(scores_grad.astype(jnp.float32), axis=0)]
  transfers between devices with their start and end apart: 8 -> 8, of which waited for: 4 -> 5; matrix products, arithmetic and copies ran while one was open for 32% -> 4% of each run, Pallas kernels for 0% -> 6%
where the time goes in v1:
time: 989 us; the launch traced here: 980 us
  waiting for transfers between devices  601 us (61%)
  blocking collectives  154 us (16%)
  Pallas kernels  143 us (14%)
  local copies, waits for them, and re-layouts  63.3 us (6%)
  between operations  14.8 us (1%)
    reduce_scatter x4, waiting for transfers between devices, scattered(): return lax.psum_scatter(value, AXES, scatter_dimension=0, tiled=True)  534 us
    unnamed x2, blocking collectives  79.4 us
    all_gather x1, blocking collectives, gathered(): return lax.all_gather(value, AXES, axis=0, tiled=True)  74.4 us
    psum x1, waiting for transfers between devices, per_device(): table_grad = lax.psum(fold_table(spread_grad), AXES)  62 us
    pallas_call x1, Pallas kernels, attend_back(): pl.pallas_call(functools.partial(attend_back_kernel, windows), grid=(HEAD...  44.3 us
    pallas_call x1, Pallas kernels, feed_forward(): pl.pallas_call(mlp_kernel, in_specs=[vmem] * 12, out_specs=[vmem] * 8, ou...  42.9 us
    pallas_call x1, Pallas kernels, attend(): pl.pallas_call(functools.partial(attend_kernel, windows), grid=(HEADS,),...  36.8 us
  transfers between devices with their start and end apart: 8, of which 5 were waited for; matrix products, arithmetic and copies ran while one was open for 4% of the time, Pallas kernels for 6%

profile of v1, /device:TPU:0, one launch (start us, length us, event | category | flops | bytes accessed | tf_op | source)
XLA Modules:
  0.0 979.6 jit_solution(11718826450026817260)
XLA Ops:
  7.2 0.7 all-gather.5.cloned.1.call-update
  8.0 0.7 all-gather.7.cloned.1.call-update
  8.7 0.7 all-gather.9.cloned.1.call-update
  9.5 6.1 concatenate.12
  15.6 0.2 dynamic-update-slice
  15.8 42.3 %all-reduce.1 = bf16[6144]{0:T(1024)(128)(2,1)S(1)} all-reduce(bf16[6144]{0:T(1024)(128)(2,1)S(1)} %dynamic-update-slice), channel_id=2, replica_groups=mesh['dp'=4,'fsdp'=8] {'dp','fsdp'}, use_global_device_ids=true, to_apply=%add.1 | all-reduce | flops 6144 | bytes 24576
  58.1 0.1 reshape.495
  58.1 0.1 slice_convert_fusion
  58.2 0.1 reshape.487
  58.3 0.1 reshape.488
  58.4 0.1 reshape.485.gain_ref
  58.5 0.1 reshape.486.shift_ref
  58.6 1.0 slice_reduce_fusion.10
  59.6 0.8 fusion.11
  60.4 0.6 concatenate.14.keyrow_ref
  61.0 1.2 reshape.473
  62.4 1.3 fusion
  63.6 4.6 reshape.475
  68.3 6.8 copy.59
  75.0 6.7 reshape.499.spread_ref
  81.8 0.1 and_convert_fusion.1
  81.8 1.2 reshape.500.keep_ref
  83.1 0.7 reshape.490.pshift_ref
  83.7 0.7 reshape.491.gain_ref
  84.4 0.7 reshape.492.shift_ref
  85.1 0.7 reshape.494.fshift2_ref
  85.7 0.7 reshape.493.fshift1_ref
  86.4 74.4 %all_gather.21.proj_ref = bf16[512,512]{1,0:T(8,128)(2,1)} all-gather(bf16[16,512]{1,0:T(8,128)(2,1)S(1)} %copy-done.5), channel_id=1, replica_groups=mesh['dp'=4,'fsdp'=8] {'dp','fsdp'}, dimensions={0}, use_global_device_ids=true | all-gather | bytes 540672 | tf_op jit(solution)/shard_map/all_gather | solution.py:475
  160.9 1.4 copy-done.1
  162.3 5.0 norm_qkv.1
  167.3 36.8 %attend.1 = (bf16[4,1536,392]{2,1,0:T(8,128)(2,1)}, bf16[4,16,392,392]{3,2,1,0:T(8,128)(2,1)}, bf16[4,392,512]{2,1,0:T(8,128)(2,1)}, bf16[4,512,392]{2,1,0:T(8,128)(2,1)}, f32[4,16,392]{2,1,0:T(8,128)}) custom-call(bf16[4,392,1536]{2,1,0:T(8,128)(2,1)} %bitcast.53, f32[16,49,735]{2,1,0:T(8,128)} %reshape.499.spread_ref, ...), custom_call_target="tpu_custom_call" | custom-call | tf_op jit(solution)/shard_map/attend/pallas_call | solution.py:157
  204.1 42.9 %feed_forward.1 = (bf16[1568,512]{1,0:T(8,128)(2,1)}, f32[1568,512]{1,0:T(8,128)}, bf16[1568,512]{1,0:T(8,128)(2,1)}, f32[512,2048]{1,0:T(8,128)}, f32[2048,512]...) custom-call(bf16[1568,512]{1,0:T(8,128)(2,1)} %bitcast.48, bf16[1568,512]{1,0:T(8,128)(2,1)} %bitcast.57, ...), custom_call_target="tpu_custom_call" | custom-call | tf_op jit(solution)/shard_map/feed_forward/pallas_call | solution.py:266
  247.0 44.3 %attend_back.1 = (bf16[4,392,1536]{2,1,0:T(8,128)(2,1)}, f32[16,49,735]{2,1,0:T(8,128)}) custom-call(bf16[4,1536,392]{2,1,0:T(8,128)(2,1)} %get-tuple-element.36.qkvt_ref, bf16[4,512,392]{2,1,0:T(8,128)(2,1)} %get-tuple-element.37.attt_ref, bf16[4,392,512]{2,1,0:T(8,128)(2,1)} %bitcast.55, f32[4,16,392]{2,1,0:T(8,128)} %get-tuple-element.39.inv_ref, ...), custom_call_target="tpu_custom_call" | custom-call | tf_op jit(solution)/shard_map/attend_back/pallas_call | solution.py:362
  291.4 2.5 copy.56
  293.9 6.4 reshape.483
  300.3 9.2 copy.57
  309.5 5.0 dot_general.9
  314.5 1.5 fusion.4
  315.9 0.1 copy.58
  316.1 0.8 reshape.484
  317.0 0.5 reduce-scatter.7.cloned.1.call-update
  317.6 14.2 %qkv_back.1 = (bf16[1568,512]{1,0:T(8,128)(2,1)}, f32[512,1536]{1,0:T(8,128)}, f32[8,1536]{1,0:T(8,128)}) custom-call(bf16[1568,512]{1,0:T(8,128)(2,1)} %bitcast.49, bf16[1568,1536]{1,0:T(8,128)(2,1)} %bitcast.54, f32[1568,512]{1,0:T(8,128)} %get-tuple-element.42.rgrad_ref, f32[1,512]{1,0:T(1,128)} %copy-done.2, f32[1,512]{1,0:T(1,128)} %copy-done.3, ...), custom_call_target="tpu_custom_call" | custom-call | tf_op jit(solution)/shard_map/qkv_back/pallas_call | solution.py:418
  331.9 0.7 reduce-scatter.11.cloned.1.call-update
  332.6 0.7 reduce-scatter.9.cloned.1.call-update
  333.4 0.9 slice_reduce_fusion.5
  334.2 0.1 reshape_squeeze.27
  334.3 0.1 reshape_squeeze.28
  334.4 0.1 reshape_squeeze.29
  334.5 0.1 reshape_squeeze.30
  334.6 0.1 reshape_squeeze.31
  334.7 0.1 reshape_squeeze.32
  334.7 0.1 reshape_squeeze.33
  334.8 0.1 reshape_squeeze.34
  334.9 0.9 slice_reduce_fusion
  335.9 0.1 concatenate.15
  336.0 37.1 %all-reduce.2 = f32[32,192]{1,0:T(8,128)S(1)} all-reduce(f32[32,192]{1,0:T(8,128)S(1)} %concatenate.15), channel_id=3, replica_groups=mesh['dp'=4,'fsdp'=8] {'dp','fsdp'}, use_global_device_ids=true, to_apply=%region_0.0.clone | all-reduce | flops 6144 | bytes 49152
  373.1 0.6 dynamic-slice_bitcast_fusion.1
  373.7 0.6 dynamic-slice_bitcast_fusion
  374.3 62.0 %all-reduce.5.cloned.1.call-done = f32[2535,16]{0,1:T(8,128)} async-done(((f32[2535,16]{0,1:T(8,128)}), f32[2535,16]{0,1:T(8,128)}) %all-reduce.5.cloned.1.call-update) | async-done | bytes 162256 | tf_op jit(solution)/shard_map/psum | solution.py:554
  436.2 139.8 %reduce-scatter.7.cloned.1.call-done = f32[16,512]{1,0:T(8,128)} async-done(((f32[512,512]{1,0:T(8,128)}), f32[16,512]{1,0:T(8,128)}) %reduce-scatter.7.cloned.1.call-update) | async-done | bytes 32784 | tf_op jit(solution)/shard_map/reduce_scatter | solution.py:479
  576.0 104.7 %reduce-scatter.5.cloned.1.call-done = f32[16,1536]{1,0:T(8,128)} async-done(((f32[512,1536]{1,0:T(8,128)}), f32[16,1536]{1,0:T(8,128)}) %reduce-scatter.5.cloned.1.call-update) | async-done | bytes 98320 | tf_op jit(solution)/shard_map/reduce_scatter | solution.py:479
  680.8 145.7 %reduce-scatter.11.cloned.1.call-done = f32[64,512]{1,0:T(8,128)} async-done(((f32[2048,512]{1,0:T(8,128)}), f32[64,512]{1,0:T(8,128)}) %reduce-scatter.11.cloned.1.call-update) | async-done | bytes 131088 | tf_op jit(solution)/shard_map/reduce_scatter | solution.py:479
  826.4 144.3 %reduce-scatter.9.cloned.1.call-done = f32[16,2048]{1,0:T(8,128)} async-done(((f32[512,2048]{1,0:T(8,128)}), f32[16,2048]{1,0:T(8,128)}) %reduce-scatter.9.cloned.1.call-update) | async-done | bytes 131088 | tf_op jit(solution)/shard_map/reduce_scatter | solution.py:479
  970.7 1.6 copy.63
  (40 shorter events, 0.6 us)
Async XLA Ops:
  7.2 153.7 %all-gather.5.cloned.1.call-start = ((), (), s32[]{:S(2)}) async-start(), calls=%async_computation.4 | async-start | bytes 1622016 | tf_op jit(solution)/shard_map/all_gather | solution.py:475
  7.9 196.2 %all-gather.7.cloned.1.call-start = ((), (), s32[]{:S(2)}) async-start(), calls=%async_computation.5 | async-start | bytes 2162688 | tf_op jit(solution)/shard_map/all_gather | solution.py:475
  8.7 195.4 %all-gather.9.cloned.1.call-start = ((), (), s32[]{:S(2)}) async-start(), calls=%async_computation.6 | async-start | bytes 2162688 | tf_op jit(solution)/shard_map/all_gather | solution.py:475
  9.4 426.8 %all-reduce.5.cloned.1.call-start = ((), (), s32[]{:S(2)}) async-start(), calls=%async_computation.8 | async-start | bytes 327680 | tf_op jit(solution)/shard_map/psum | solution.py:554
  58.5 102.4 %copy-start.2 = (f32[1,512]{1,0:T(1,128)}, f32[1,512]{1,0:T(1,128)S(1)}, u32[]{:S(2)}) copy-start(f32[1,512]{1,0:T(1,128)S(1)} %reshape.485.gain_ref) | copy-start | bytes 6148
  58.6 102.3 %copy-start.3 = (f32[1,512]{1,0:T(1,128)}, f32[1,512]{1,0:T(1,128)S(1)}, u32[]{:S(2)}) copy-start(f32[1,512]{1,0:T(1,128)S(1)} %reshape.486.shift_ref) | copy-start | bytes 6148
  75.0 6.7 copy-start.6
  75.0 6.7 copy-start.7
  75.0 6.7 copy-start.8
  75.0 11.4 %copy-start.5 = (bf16[16,512]{1,0:T(8,128)(2,1)S(1)}, bf16[16,512]{1,0:T(8,128)(2,1)}, u32[]{:S(2)}) copy-start(bf16[16,512]{1,0:T(8,128)(2,1)} %param.31) | copy-start | bytes 49156
  75.0 85.8 %copy-start = (bf16[4,392,512]{2,1,0:T(8,128)(2,1)S(1)}, bf16[4,392,512]{2,1,0:T(8,128)(2,1)}, u32[]{:S(2)}) copy-start(bf16[4,392,512]{2,1,0:T(8,128)(2,1)} %param.22) | copy-start | bytes 4816900
  160.9 1.4 copy-start.1
  309.5 5.0 copy-start.4
  317.0 259.1 %reduce-scatter.7.cloned.1.call-start = ((), (), s32[]{:S(2)}) async-start(), calls=%async_computation.9 | async-start | bytes 1081344 | tf_op jit(solution)/shard_map/reduce_scatter | solution.py:479
  317.6 363.2 %reduce-scatter.5.cloned.1.call-start = ((), (), s32[]{:S(2)}) async-start(), calls=%async_computation.7 | async-start | bytes 3244032 | tf_op jit(solution)/shard_map/reduce_scatter | solution.py:479
  331.8 494.6 %reduce-scatter.11.cloned.1.call-start = ((), (), s32[]{:S(2)}) async-start(), calls=%async_computation.11 | async-start | bytes 4325376 | tf_op jit(solution)/shard_map/reduce_scatter | solution.py:479
  332.6 1.9 copy-start.9
  332.6 638.1 %reduce-scatter.9.cloned.1.call-start = ((), (), s32[]{:S(2)}) async-start(), calls=%async_computation.10 | async-start | bytes 4325376 | tf_op jit(solution)/shard_map/reduce_scatter | solution.py:479
Sparse Core Ops, SparseCore 0:
  11.0 57.8 all-gather.4
  71.8 56.6 all-gather.6
  131.5 55.6 all-gather.8
  317.1 119.1 all-reduce.4
  438.9 137.0 reduce-scatter.6
  582.8 97.9 reduce-scatter.4
  683.7 142.6 reduce-scatter.10
  829.4 141.3 reduce-scatter.8
